TPU v7x, 32 devices: a whole 2x2x4 slice. The times are simulated.
32 devices in a mesh: parts: 2 (over x), sta: 16 (over z, y, core).
Axes of the slice: x: 2, y: 2, z: 4, core: 2. Of those that a mesh axis runs over, the one named last changes fastest.
Arguments:
- raw_traces: bfloat16 [512, 16384], P('parts', 'sta'), parts along dimension 0, may hold values from -6 to 6
- filter_taps: bfloat16 [256], replicated, may hold values from -0.375 to 0.375
- station_order: int32 [512], P('parts'), parts along dimension 0, may hold values from 0 to 255, each once
- window_starts: int32 [32], P('parts'), parts along dimension 0, may hold values from 0 to 2048, as said below
- pairing: int32 [4, 16], replicated, may hold values from 0 to 15, as said below
Outputs:
- correlation: float32 [4, 512, 16, 256], P(None, ('parts', 'sta')), parts along dimension 1
There are 2 independent parts, one for each index of `parts`. A program takes and returns all parts, laid end to end along the dimension named above; an argument that names none is the same for every part. Nothing has to cross between parts.
Inputs may be any that keep to these rules, and one draw needn't show every extreme that they name: Each station appears once; block b holds the stations station_order[b * 16 + j], j < 16. `window_starts`: starts never fall; the first is 0 and the last is 2048; consecutive starts differ by at most 273. Row r is one round of a single round-robin tournament over the 16 blocks: pairing[r, pairing[r, b]] = b, pairing[r, b] != b, and no two rows pair the same two blocks.
All inputs are finite; a program needn't handle non-finite values.
Results may differ from a plain program's by a relative error of at most 0.0049.
Values may be sent and summed in bfloat16 or wider, within the bound.
A program may use at most 128 MiB of HBM per device.

v0:
```python
import math
import jax
import jax.numpy as jnp
from jax import lax
from jax.sharding import PartitionSpec as P

DEC = 4
TAPS = 256
SEG = 2048
BAND = 64
LAGS = 256
ROUNDS = 4
BINS = 1024


def decimate(signal, leading, filter_taps, factor):
    row_count, length = signal.shape
    outputs = length // factor
    per_tile = math.gcd(outputs, 128)
    tile_span = per_tile * factor
    margin = leading.shape[1]
    pieces = 1 + (margin + tile_span - 1) // tile_span
    tile_count = outputs // per_tile
    padded = jnp.concatenate(
        [leading, signal, jnp.zeros((row_count, (pieces - 1) * tile_span - margin), signal.dtype)],
        axis=1,
    )
    tap_count = filter_taps.shape[0]
    positions = jnp.arange(pieces * tile_span, dtype=jnp.int32)[:, None]
    column = jnp.arange(per_tile, dtype=jnp.int32)[None, :]
    tap_index = column * factor + tap_count - 1 - positions
    inside = (tap_index >= 0) & (tap_index < tap_count)
    banded = jnp.where(
        inside,
        jnp.take(filter_taps, jnp.clip(tap_index, 0, tap_count - 1)),
        jnp.zeros((), filter_taps.dtype),
    )
    summed = jnp.zeros((row_count, tile_count, per_tile), jnp.float32)
    for section_index in range(pieces):
        segment = padded[:, section_index * tile_span : section_index * tile_span + length].reshape(
            row_count, tile_count, tile_span
        )
        summed = summed + jnp.einsum(
            "rtu,ui->rti",
            segment,
            banded[section_index * tile_span : (section_index + 1) * tile_span],
            preferred_element_type=jnp.float32,
        )
    return summed.reshape(row_count, outputs)


def dft_matrix(seg_length, bin_count):
    sample = jnp.arange(seg_length, dtype=jnp.int32)
    frequency = jnp.arange(bin_count, dtype=jnp.int32)
    angles = (frequency[:, None] * sample[None, :] % seg_length).astype(jnp.float32) * (
        2.0 * math.pi / seg_length
    )
    taper_curve = 0.5 - 0.5 * jnp.cos(sample.astype(jnp.float32) * (2.0 * math.pi / seg_length))
    joined = jnp.concatenate(
        [jnp.cos(angles) * taper_curve[None, :], -jnp.sin(angles) * taper_curve[None, :]], axis=0
    )
    return joined.astype(jnp.bfloat16)


def lag_matrix(seg_length, bin_count, lag_count, window_count):
    frequency = jnp.arange(bin_count, dtype=jnp.int32)
    lag_offset = jnp.arange(lag_count, dtype=jnp.int32) - lag_count // 2 + seg_length
    angles = (frequency[:, None] * lag_offset[None, :] % seg_length).astype(jnp.float32) * (
        2.0 * math.pi / seg_length
    )
    normalizer = 1.0 / math.sqrt(bin_count * window_count)
    return jnp.stack([jnp.cos(angles) * normalizer, -jnp.sin(angles) * normalizer]).astype(
        jnp.bfloat16
    )


def whiten_flat(spectrum, band_width):
    halves, bin_count, columns = spectrum.shape
    grouped = spectrum.reshape(halves, bin_count // band_width, band_width, columns)
    band_level = jnp.sum(grouped * grouped, axis=(0, 2)) / (2 * band_width)
    scaled = grouped * (1.0 / jnp.sqrt(band_level + 1e-06))[None, :, None]
    return scaled.reshape(spectrum.shape).astype(jnp.bfloat16)


def cross_spectra(left_spec, right_spec):
    turned = jnp.stack([right_spec, jnp.stack([-right_spec[1], right_spec[0]])])
    return jnp.einsum("cfws,kcfwt->kfst", left_spec, turned, preferred_element_type=jnp.float32)


def body(raw_traces, filter_taps, station_order, window_starts, pairing):
    members = lax.axis_size("sta")
    station_count, local_time = raw_traces.shape
    block_size = station_count // members
    margin = TAPS - DEC
    ordered = jnp.take(raw_traces, station_order, axis=0)
    gathered = lax.all_to_all(ordered, "sta", split_axis=0, concat_axis=1, tiled=True)
    leading = jnp.zeros((block_size, margin), gathered.dtype)
    low_rate = decimate(gathered, leading, filter_taps, DEC).astype(jnp.bfloat16)
    window_count = window_starts.shape[0]
    windows = jax.vmap(
        lambda first_sample: lax.dynamic_slice_in_dim(low_rate, first_sample, SEG, 1)
    )(window_starts)
    windows = windows.reshape(window_count * block_size, SEG)
    spectrum = lax.dot_general(
        dft_matrix(SEG, BINS), windows, (((1,), (1,)), ((), ())), preferred_element_type=jnp.float32
    )
    whitened = whiten_flat(spectrum.reshape(2, BINS, window_count * block_size), BAND)
    by_bin = lax.all_to_all(whitened[None], "sta", split_axis=2, concat_axis=0, tiled=True)
    lag_table = lag_matrix(SEG, BINS, LAGS, window_count)
    own_spec = whitened.reshape(2, BINS, window_count, block_size)
    collected = []
    for round_index in range(ROUNDS):
        picked = jnp.take(by_bin, pairing[round_index], axis=0)
        partner_spec = lax.all_to_all(picked, "sta", split_axis=0, concat_axis=2, tiled=True)
        partner_spec = partner_spec.reshape(2, BINS, window_count, block_size)
        cross_spec = cross_spectra(own_spec, partner_spec).astype(jnp.bfloat16)
        collected.append(cross_spec.reshape(2, BINS, block_size * block_size))
    correlated = jnp.einsum(
        "rkfp,kfl->rpl", jnp.stack(collected), lag_table, preferred_element_type=jnp.float32
    )
    return correlated.reshape(ROUNDS, block_size, block_size, LAGS)


def solution(mesh):
    return jax.shard_map(
        body,
        mesh=mesh,
        in_specs=(P("parts", "sta"), P(), P("parts"), P("parts"), P()),
        out_specs=P(None, ("parts", "sta"), None, None),
        check_vma=False,
    )
```

profile of v0, /device:TPU:0, one launch (start us, length us, event | category | flops | bytes accessed | tf_op | source)
XLA Modules:
  0.0 1280.5 jit_solution(12925101330786375420)
XLA Ops:
  3.6 7.4 all-to-all-start
  11.3 35.5 %multiply_convert_fusion.1 = (bf16[1024,2048]{1,0:T(8,128)(2,1)}, bf16[1024,2048]{1,0:T(8,128)(2,1)}) fusion(f32[2048]{0:T(1024)S(1)} %multiply_subtract_fusion), kind=kLoop, calls=%fused_computation.20 | loop fusion | flops 39845888 | bytes 8396800 | tf_op jit(solution)/shard_map/convert.2
  46.8 764.8 %gather_fusion.1 = bf16[131072]{0:T(1024)(128)(2,1)S(1)} fusion(bf16[256]{0:T(256)(128)(2,1)S(1)} %copy-done.2, s32[131072]{0:T(1024)S(1)} %fusion.28), kind=kCustom, calls=%fused_computation.5 | custom fusion | bytes 1048576 | tf_op jit(solution)/shard_map/jit(_take)/gather | solution.py:35
  812.0 8.4 pad_maximum_fusion
  821.7 21.5 %while.1 = (s32[]{:T(128)}, bf16[16,4096]{1,0:T(8,128)(2,1)S(1)}, s32[16,2]{0,1:T(2,128)S(1)}, bf16[16,16,2048]{2,1,0:T(8,128)(2,1)S(1)}, s32[]{:T(128)}) while((s32[]{:T(128)}, bf16[16,4096]{1,0:T(8,128)(2,1)S(1)}, s32[16,2]{0,1:T(2,128)S(1)}, bf16[16,16,2048]{2,1,0:T(8,128)(2,1)S(1)}, s32[]{:T(128)}) %tuple.38), condition=%wide.while_cond, body=%wide.while_body.sunk | while | flops 2 | bytes 131169 | solution.py:101
  843.3 5.8 multiply_reduce_fusion
  851.4 6.0 all-to-all-start.1
  857.5 22.9 %all-to-all-done.1 = bf16[1,2,1024,256]{3,1,0,2:T(2,128)(2,1)S(1)} async-done(((bf16[1,2,1024,256]{3,1,0,2:T(2,128)(2,1)}), bf16[1,2,1024,256]{3,1,0,2:T(2,128)(2,1)S(1)}, u32[]{:S(2)}, u32[]{:S(2)}) %all-to-all-start.1) | async-done | bytes 1048608 | tf_op jit(solution)/shard_map/all_to_all | solution.py:108
  886.7 6.9 all-to-all-start.2
  895.2 2.4 broadcast_select_fusion.2
  897.6 19.0 %all-to-all-done.2 = bf16[16,2,64,256]{3,2,1,0:T(8,128)(2,1)} async-done(((bf16[16,2,64,256]{3,2,1,0:T(8,128)(2,1)}), bf16[16,2,64,256]{3,2,1,0:T(8,128)(2,1)}, u32[]{:S(2)}, u32[]{:S(2)}) %all-to-all-start.2) | async-done | bytes 1048608 | tf_op jit(solution)/shard_map/all_to_all | solution.py:114
  916.6 7.2 all-to-all-start.3
  927.7 19.0 %all-to-all-done.3 = bf16[16,2,64,256]{3,2,1,0:T(8,128)(2,1)} async-done(((bf16[16,2,64,256]{3,2,1,0:T(8,128)(2,1)}), bf16[16,2,64,256]{3,2,1,0:T(8,128)(2,1)}, u32[]{:S(2)}, u32[]{:S(2)}) %all-to-all-start.3) | async-done | bytes 1048608 | tf_op jit(solution)/shard_map/all_to_all | solution.py:114
  946.8 6.9 all-to-all-start.4
  955.3 2.4 broadcast_select_fusion
  957.6 19.0 %all-to-all-done.4 = bf16[16,2,64,256]{3,2,1,0:T(8,128)(2,1)} async-done(((bf16[16,2,64,256]{3,2,1,0:T(8,128)(2,1)}), bf16[16,2,64,256]{3,2,1,0:T(8,128)(2,1)}, u32[]{:S(2)}, u32[]{:S(2)}) %all-to-all-start.4) | async-done | bytes 1048608 | tf_op jit(solution)/shard_map/all_to_all | solution.py:114
  976.7 6.9 all-to-all-start.5
  983.6 5.5 multiply_convert_fusion.4
  989.0 2.8 copy.109
  991.8 3.2 convert_element_type.96
  995.1 12.1 copy.132
  1007.2 3.8 copy.106
  1011.0 3.8 copy.113
  1014.8 3.8 copy.119
  1024.5 2.8 copy.125
  1030.7 4.1 stack_reshape.24
  1036.3 32.0 %copy.110 = bf16[2,2,1024,16,16]{3,4,1,0,2:T(8,128)(2,1)} copy(bf16[2,2,1024,16,16]{2,4,3,1,0:T(8,128)(2,1)S(1)} %pad_maximum_fusion.1) | data formatting | bytes 4194304 | tf_op jit(solution)/shard_map/stack | solution.py:86
  1068.3 13.4 %fusion.6 = bf16[2,1024,16,16]{2,3,0,1:T(8,128)(2,1)} fusion(bf16[2,2,1024,16,16]{3,4,1,0,2:T(8,128)(2,1)} %copy.110, bf16[2,1024,16,16,1]{3,2,0,4,1:T(8,128)(2,1)} %copy.132), kind=kOutput, calls=%fused_computation.24 | convolution fusion | flops 34078720 | bytes 4194304 | tf_op jit(solution)/shard_map/cfws,kcfwt->kfst/dot_general | solution.py:87
  1081.7 10.1 copy.112
  1091.8 2.9 copy.114
  1094.7 2.6 neg.69
  1097.3 2.9 copy.115
  1100.2 2.6 slice.77
  1107.8 23.2 %copy.116 = bf16[2,2,1024,16,16]{3,4,1,0,2:T(8,128)(2,1)} copy(bf16[2,2,1024,16,16]{2,4,3,1,0:T(8,128)(2,1)S(1)} %pad_maximum_fusion.2) | data formatting | bytes 4194304 | tf_op jit(solution)/shard_map/stack | solution.py:86
  1131.1 13.4 %fusion.7 = bf16[2,1024,16,16]{2,3,0,1:T(8,128)(2,1)} fusion(bf16[2,2,1024,16,16]{3,4,1,0,2:T(8,128)(2,1)} %copy.116, bf16[2,1024,16,16,1]{3,2,0,4,1:T(8,128)(2,1)} %copy.132), kind=kOutput, calls=%fused_computation.25 | convolution fusion | flops 34078720 | bytes 4194304 | tf_op jit(solution)/shard_map/cfws,kcfwt->kfst/dot_general | solution.py:87
  1144.5 10.3 copy.118
  1154.8 2.9 copy.120
  1157.7 2.6 neg.71
  1160.3 2.9 copy.121
  1163.2 2.6 slice.81
  1170.8 23.2 %copy.122 = bf16[2,2,1024,16,16]{3,4,1,0,2:T(8,128)(2,1)} copy(bf16[2,2,1024,16,16]{2,4,3,1,0:T(8,128)(2,1)S(1)} %pad_maximum_fusion.3) | data formatting | bytes 4194304 | tf_op jit(solution)/shard_map/stack | solution.py:86
  1194.0 13.4 %fusion.8 = bf16[2,1024,16,16]{2,3,0,1:T(8,128)(2,1)} fusion(bf16[2,2,1024,16,16]{3,4,1,0,2:T(8,128)(2,1)} %copy.122, bf16[2,1024,16,16,1]{3,2,0,4,1:T(8,128)(2,1)} %copy.132), kind=kOutput, calls=%fused_computation.26 | convolution fusion | flops 34078720 | bytes 4194304 | tf_op jit(solution)/shard_map/cfws,kcfwt->kfst/dot_general | solution.py:87
  1207.4 10.2 copy.124
  1225.2 2.5 stack_reshape.30
  1229.2 23.2 %copy.128 = bf16[2,2,1024,16,16]{3,4,1,0,2:T(8,128)(2,1)} copy(bf16[2,2,1024,16,16]{2,4,3,1,0:T(8,128)(2,1)S(1)} %pad_maximum_fusion.4) | data formatting | bytes 4194304 | tf_op jit(solution)/shard_map/stack | solution.py:86
  1252.5 13.4 %fusion.9 = bf16[2,1024,16,16]{2,3,0,1:T(8,128)(2,1)} fusion(bf16[2,2,1024,16,16]{3,4,1,0,2:T(8,128)(2,1)} %copy.128, bf16[2,1024,16,16,1]{3,2,0,4,1:T(8,128)(2,1)} %copy.132), kind=kOutput, calls=%fused_computation.27 | convolution fusion | flops 34078720 | bytes 4194304 | tf_op jit(solution)/shard_map/cfws,kcfwt->kfst/dot_general | solution.py:87
  1265.9 10.1 copy.130
  1276.1 4.0 fusion.10
  (132 shorter events, 72.3 us)
Async XLA Ops:
  0.0 1.5 copy-start
  0.0 46.8 %copy-start.11 = (s32[16]{0:T(128)S(1)}, s32[16]{0:T(128)}, u32[]{:S(2)}) copy-start(s32[16]{0:T(128)} %param.10) | copy-start | bytes 196
  0.0 46.8 %copy-start.2 = (bf16[256]{0:T(256)(128)(2,1)S(1)}, bf16[256]{0:T(256)(128)(2,1)}, u32[]{:S(2)}) copy-start(bf16[256]{0:T(256)(128)(2,1)} %param.8) | copy-start | bytes 1540
  3.6 816.7 %all-to-all-start = ((bf16[16,16,1024]{2,1,0:T(8,128)(2,1)}), bf16[16,16,1024]{2,1,0:T(8,128)(2,1)S(1)}, u32[]{:S(2)}, u32[]{:S(2)}) async-start(bf16[16,16,1024]{2,1,0:T(8,128)(2,1)} %broadcast_select_fusion.4), calls=%async_computation | async-start | bytes 1048576 | tf_op jit(solution)/shard_map/all_to_all | solution.py:96
  843.3 14.2 %copy-start.10 = (s32[4,16]{1,0:T(4,128)S(1)}, s32[4,16]{1,0:T(4,128)}, u32[]{:S(2)}) copy-start(s32[4,16]{1,0:T(4,128)} %param.11) | copy-start | bytes 772
  851.4 29.0 %all-to-all-start.1 = ((bf16[1,2,1024,256]{3,1,0,2:T(2,128)(2,1)}), bf16[1,2,1024,256]{3,1,0,2:T(2,128)(2,1)S(1)}, u32[]{:S(2)}, u32[]{:S(2)}) async-start(bf16[1,2,1024,256]{3,1,0,2:T(2,128)(2,1)} %copy.103), calls=%async_computation.1 | async-start | bytes 2097152 | tf_op jit(solution)/shard_map/all_to_all | solution.py:108
  880.4 1.0 copy-start.6
  886.7 29.9 %all-to-all-start.2 = ((bf16[16,2,64,256]{3,2,1,0:T(8,128)(2,1)}), bf16[16,2,64,256]{3,2,1,0:T(8,128)(2,1)}, u32[]{:S(2)}, u32[]{:S(2)}) async-start(bf16[16,2,64,256]{3,2,1,0:T(8,128)(2,1)} %broadcast_select_fusion.3), calls=%async_computation.2 | async-start | bytes 2097152 | tf_op jit(solution)/shard_map/all_to_all | solution.py:114
  916.6 30.2 %all-to-all-start.3 = ((bf16[16,2,64,256]{3,2,1,0:T(8,128)(2,1)}), bf16[16,2,64,256]{3,2,1,0:T(8,128)(2,1)}, u32[]{:S(2)}, u32[]{:S(2)}) async-start(bf16[16,2,64,256]{3,2,1,0:T(8,128)(2,1)} %broadcast_select_fusion.2), calls=%async_computation.3 | async-start | bytes 2097152 | tf_op jit(solution)/shard_map/all_to_all | solution.py:114
  946.8 29.9 %all-to-all-start.4 = ((bf16[16,2,64,256]{3,2,1,0:T(8,128)(2,1)}), bf16[16,2,64,256]{3,2,1,0:T(8,128)(2,1)}, u32[]{:S(2)}, u32[]{:S(2)}) async-start(bf16[16,2,64,256]{3,2,1,0:T(8,128)(2,1)} %broadcast_select_fusion.1), calls=%async_computation.4 | async-start | bytes 2097152 | tf_op jit(solution)/shard_map/all_to_all | solution.py:114
  976.7 47.8 %all-to-all-start.5 = ((bf16[16,2,64,256]{3,2,1,0:T(8,128)(2,1)}), bf16[16,2,64,256]{3,2,1,0:T(8,128)(2,1)S(1)}, u32[]{:S(2)}, u32[]{:S(2)}) async-start(bf16[16,2,64,256]{3,2,1,0:T(8,128)(2,1)} %broadcast_select_fusion), calls=%async_computation.5 | async-start | bytes 2097152 | tf_op jit(solution)/shard_map/all_to_all | solution.py:114
  1081.7 21.1 %copy-start.5 = (bf16[1,2,16,64,256]{3,2,4,1,0:T(8,128)(2,1)S(1)}, bf16[1,2,16,64,256]{3,2,4,1,0:T(8,128)(2,1)}, u32[]{:S(2)}) copy-start(bf16[1,2,16,64,256]{3,2,4,1,0:T(8,128)(2,1)} %copy.113) | copy-start | bytes 3145732
  1144.5 21.3 %copy-start.4 = (bf16[1,2,16,64,256]{3,2,4,1,0:T(8,128)(2,1)S(1)}, bf16[1,2,16,64,256]{3,2,4,1,0:T(8,128)(2,1)}, u32[]{:S(2)}) copy-start(bf16[1,2,16,64,256]{3,2,4,1,0:T(8,128)(2,1)} %copy.119) | copy-start | bytes 3145732
  1207.4 17.8 %copy-start.3 = (bf16[1,2,16,64,256]{3,2,4,1,0:T(8,128)(2,1)S(1)}, bf16[1,2,16,64,256]{3,2,4,1,0:T(8,128)(2,1)}, u32[]{:S(2)}) copy-start(bf16[1,2,16,64,256]{3,2,4,1,0:T(8,128)(2,1)} %copy.125) | copy-start | bytes 3145732
  1265.9 10.1 copy-start.7
  1265.9 10.1 copy-start.8
  1265.9 10.1 copy-start.9
  1276.0 4.0 copy-start.1
where the time goes:
time: 1290 us; the launch traced here: 1280 us
  local copies, waits for them, and re-layouts  1020 us (79%)
  waiting for transfers between devices  80 us (6%)
  other arithmetic  76.3 us (6%)
  matrix products  64.1 us (5%)
  starting transfers between devices  41.3 us (3%)
    gather x1, local copies, waits for them, and re-layouts, decimate(): jnp.take(filter_taps, jnp.clip(tap_index, 0, tap_count - 1))  765 us
    another operation x8, local copies, waits for them, and re-layouts, cross_spectra(): turned = jnp.stack([right_spec, jnp.stack([-right_spec[1], right_spec[0]])])  113 us
    all_to_all x4, waiting for transfers between devices, body(): lax.all_to_all(picked, 'sta', split_axis=0, concat_axis=2, tiled=True)  57.1 us
    dot_general x4, matrix products, cross_spectra(): jnp.einsum('cfws,kcfwt->kfst', left_spec, turned, preferred_element_type=...  53.7 us
    another operation x2, other arithmetic  41 us
    convert_element_type x4, local copies, waits for them, and re-layouts, body(): cross_spec = cross_spectra(own_spec, partner_spec).astype(jnp.bfloat16)  40.7 us
    all_to_all x4, starting transfers between devices, body(): lax.all_to_all(picked, 'sta', split_axis=0, concat_axis=2, tiled=True)  27.9 us
  transfers between devices with their start and end apart: 6, of which 4 were waited for; matrix products, arithmetic and copies ran while one was open for 67% of the time, Pallas kernels for 0%

commit v1 on v0

--- a/solution.py
+++ b/solution.py
@@ -11,6 +11,18 @@
 LAGS = 256
 ROUNDS = 4
 BINS = 1024
+
+
+def cut_along(x, dim, devices):
+    lengths = x.shape
+    blocks = x.reshape(*lengths[:dim], devices, lengths[dim] // devices, *lengths[dim + 1 :])
+    return jnp.moveaxis(blocks, dim, 0)
+
+
+def laid_out(blocks, dim):
+    shape = list(blocks.shape[1:])
+    shape[dim] *= blocks.shape[0]
+    return jnp.moveaxis(blocks, 0, dim).reshape(shape)
 
 
 def decimate(signal, leading, filter_taps, factor):
@@ -105,7 +117,14 @@
         dft_matrix(SEG, BINS), windows, (((1,), (1,)), ((), ())), preferred_element_type=jnp.float32
     )
     whitened = whiten_flat(spectrum.reshape(2, BINS, window_count * block_size), BAND)
-    by_bin = lax.all_to_all(whitened[None], "sta", split_axis=2, concat_axis=0, tiled=True)
+    size, position = (lax.axis_size("sta"), lax.axis_index("sta"))
+    parts = cut_along(whitened[None], 2, size)
+    outs = [parts[position]]
+    for step in range(1, size):
+        sent = parts[(position + step) % size]
+        outs.append(lax.ppermute(sent, "sta", [(i, (i + step) % size) for i in range(size)]))
+    parts = jnp.stack(outs)[(position - jnp.arange(size)) % size]
+    by_bin = laid_out(parts, 0)
     lag_table = lag_matrix(SEG, BINS, LAGS, window_count)
     own_spec = whitened.reshape(2, BINS, window_count, block_size)
     collected = []

time: 1290 us -> 1300 us (level)
  waiting for transfers between devices: 80 us -> 66.7 us
    all_to_all x1 -> x0, waiting for transfers between devices: 22.9 us -> none  [body(): lax.all_to_all(whitened[None], 'sta', split_axis=2, concat_axis=0, tiled=...]
    ppermute x0 -> x15, starting transfers between devices: none -> 19.8 us  [body(): lax.ppermute(sent, 'sta', [(i, (i + step) % size) for i in range(size)])]
    gather x48 -> x49, local copies, waits for them, and re-layouts: 21.2 us -> 33 us
  transfers between devices with their start and end apart: 6 -> 20, of which waited for: 4 -> 7; matrix products, arithmetic and copies ran while one was open for 67% -> 67% of each run, Pallas kernels for 0% -> 0%
where the time goes in v1:
time: 1300 us; the launch traced here: 1290 us
  local copies, waits for them, and re-layouts  1030 us (79%)
  other arithmetic  77.1 us (6%)
  waiting for transfers between devices  66.7 us (5%)
  matrix products  64.4 us (5%)
  starting transfers between devices  53.9 us (4%)
    gather x1, local copies, waits for them, and re-layouts, decimate(): jnp.take(filter_taps, jnp.clip(tap_index, 0, tap_count - 1))  765 us
    another operation x8, local copies, waits for them, and re-layouts, cross_spectra(): turned = jnp.stack([right_spec, jnp.stack([-right_spec[1], right_spec[0]])])  113 us
    all_to_all x4, waiting for transfers between devices, body(): lax.all_to_all(picked, 'sta', split_axis=0, concat_axis=2, tiled=True)  57.1 us
    dot_general x4, matrix products, cross_spectra(): jnp.einsum('cfws,kcfwt->kfst', left_spec, turned, preferred_element_type=...  53.7 us
    another operation x2, other arithmetic  40.9 us
    convert_element_type x4, local copies, waits for them, and re-layouts, body(): cross_spec = cross_spectra(own_spec, partner_spec).astype(jnp.bfloat16)  40.6 us
    gather x48, local copies, waits for them, and re-layouts  31.2 us
    all_to_all x4, starting transfers between devices, body(): lax.all_to_all(picked, 'sta', split_axis=0, concat_axis=2, tiled=True)  26.7 us
  transfers between devices with their start and end apart: 20, of which 7 were waited for; matrix products, arithmetic and copies ran while one was open for 67% of the time, Pallas kernels for 0%

profile of v1, /device:TPU:0, one launch (start us, length us, event | category | flops | bytes accessed | tf_op | source)
XLA Modules:
  0.0 1289.5 jit_solution(5398070227189518521)
XLA Ops:
  3.6 7.4 all-to-all-start
  12.2 35.5 %multiply_convert_fusion.1 = (bf16[1024,2048]{1,0:T(8,128)(2,1)}, bf16[1024,2048]{1,0:T(8,128)(2,1)}) fusion(f32[2048]{0:T(1024)S(1)} %multiply_subtract_fusion), kind=kLoop, calls=%fused_computation.21 | loop fusion | flops 39845888 | bytes 8396800 | tf_op jit(solution)/shard_map/convert.2
  47.8 764.8 %gather_fusion.1 = bf16[131072]{0:T(1024)(128)(2,1)S(1)} fusion(bf16[256]{0:T(256)(128)(2,1)S(1)} %copy-done.2, s32[131072]{0:T(1024)S(1)} %fusion.28), kind=kCustom, calls=%fused_computation.5 | custom fusion | bytes 1048576 | tf_op jit(solution)/shard_map/jit(_take)/gather | solution.py:47
  812.9 8.4 pad_maximum_fusion
  822.7 31.2 %while.1 = (s32[]{:T(128)}, bf16[16,4096]{1,0:T(8,128)(2,1)S(1)}, s32[16,2]{0,1:T(2,128)S(1)}, bf16[16,16,2048]{2,1,0:T(8,128)(2,1)}, s32[]{:T(128)}) while((s32[]{:T(128)}, bf16[16,4096]{1,0:T(8,128)(2,1)S(1)}, s32[16,2]{0,1:T(2,128)S(1)}, bf16[16,16,2048]{2,1,0:T(8,128)(2,1)}, s32[]{:T(128)}) %tuple.52), condition=%wide.while_cond, body=%wide.while_body.sunk | while | flops 2 | bytes 132185 | solution.py:113
  853.9 6.1 multiply_reduce_fusion
  867.8 4.0 collective-permute-start.6
  872.8 6.5 collective-permute-done.4
  879.9 3.1 collective-permute-start.11
  883.9 2.7 collective-permute-start.13
  896.9 6.0 all-to-all-start.1
  906.9 19.0 %all-to-all-done.1 = bf16[16,2,64,256]{3,2,1,0:T(8,128)(2,1)} async-done(((bf16[16,2,64,256]{3,2,1,0:T(8,128)(2,1)}), bf16[16,2,64,256]{3,2,1,0:T(8,128)(2,1)}, u32[]{:S(2)}, u32[]{:S(2)}) %all-to-all-start.1) | async-done | bytes 1048608 | tf_op jit(solution)/shard_map/all_to_all | solution.py:133
  925.9 6.9 all-to-all-start.2
  936.8 19.0 %all-to-all-done.2 = bf16[16,2,64,256]{3,2,1,0:T(8,128)(2,1)} async-done(((bf16[16,2,64,256]{3,2,1,0:T(8,128)(2,1)}), bf16[16,2,64,256]{3,2,1,0:T(8,128)(2,1)}, u32[]{:S(2)}, u32[]{:S(2)}) %all-to-all-start.2) | async-done | bytes 1048608 | tf_op jit(solution)/shard_map/all_to_all | solution.py:133
  955.8 6.9 all-to-all-start.3
  966.7 19.0 %all-to-all-done.3 = bf16[16,2,64,256]{3,2,1,0:T(8,128)(2,1)} async-done(((bf16[16,2,64,256]{3,2,1,0:T(8,128)(2,1)}), bf16[16,2,64,256]{3,2,1,0:T(8,128)(2,1)}, u32[]{:S(2)}, u32[]{:S(2)}) %all-to-all-start.3) | async-done | bytes 1048608 | tf_op jit(solution)/shard_map/all_to_all | solution.py:133
  985.7 6.9 all-to-all-start.4
  992.6 5.5 multiply_convert_fusion.4
  998.1 2.8 copy.71
  1000.9 3.2 convert_element_type.87
  1004.2 12.1 copy.94
  1016.2 3.8 copy.68
  1020.0 3.8 copy.75
  1023.9 3.8 copy.81
  1033.6 2.9 copy.87
  1039.8 4.1 stack_reshape.24
  1045.4 32.0 %copy.72 = bf16[2,2,1024,16,16]{3,4,1,0,2:T(8,128)(2,1)} copy(bf16[2,2,1024,16,16]{2,4,3,1,0:T(8,128)(2,1)S(1)} %pad_maximum_fusion.1) | data formatting | bytes 4194304 | tf_op jit(solution)/shard_map/stack | solution.py:98
  1077.4 13.4 %fusion.6 = bf16[2,1024,16,16]{2,3,0,1:T(8,128)(2,1)} fusion(bf16[2,2,1024,16,16]{3,4,1,0,2:T(8,128)(2,1)} %copy.72, bf16[2,1024,16,16,1]{3,2,0,4,1:T(8,128)(2,1)} %copy.94), kind=kOutput, calls=%fused_computation.25 | convolution fusion | flops 34078720 | bytes 4194304 | tf_op jit(solution)/shard_map/cfws,kcfwt->kfst/dot_general | solution.py:99
  1090.8 10.1 copy.74
  1100.9 2.9 copy.76
  1103.8 2.6 neg.69
  1106.4 2.9 copy.77
  1109.3 2.6 slice.77
  1116.9 23.2 %copy.78 = bf16[2,2,1024,16,16]{3,4,1,0,2:T(8,128)(2,1)} copy(bf16[2,2,1024,16,16]{2,4,3,1,0:T(8,128)(2,1)S(1)} %pad_maximum_fusion.2) | data formatting | bytes 4194304 | tf_op jit(solution)/shard_map/stack | solution.py:98
  1140.2 13.4 %fusion.7 = bf16[2,1024,16,16]{2,3,0,1:T(8,128)(2,1)} fusion(bf16[2,2,1024,16,16]{3,4,1,0,2:T(8,128)(2,1)} %copy.78, bf16[2,1024,16,16,1]{3,2,0,4,1:T(8,128)(2,1)} %copy.94), kind=kOutput, calls=%fused_computation.26 | convolution fusion | flops 34078720 | bytes 4194304 | tf_op jit(solution)/shard_map/cfws,kcfwt->kfst/dot_general | solution.py:99
  1153.6 10.3 copy.80
  1163.9 2.9 copy.82
  1166.8 2.6 neg.71
  1169.4 2.9 copy.83
  1172.3 2.6 slice.81
  1179.9 23.2 %copy.84 = bf16[2,2,1024,16,16]{3,4,1,0,2:T(8,128)(2,1)} copy(bf16[2,2,1024,16,16]{2,4,3,1,0:T(8,128)(2,1)S(1)} %pad_maximum_fusion.3) | data formatting | bytes 4194304 | tf_op jit(solution)/shard_map/stack | solution.py:98
  1203.1 13.4 %fusion.8 = bf16[2,1024,16,16]{2,3,0,1:T(8,128)(2,1)} fusion(bf16[2,2,1024,16,16]{3,4,1,0,2:T(8,128)(2,1)} %copy.84, bf16[2,1024,16,16,1]{3,2,0,4,1:T(8,128)(2,1)} %copy.94), kind=kOutput, calls=%fused_computation.27 | convolution fusion | flops 34078720 | bytes 4194304 | tf_op jit(solution)/shard_map/cfws,kcfwt->kfst/dot_general | solution.py:99
  1216.5 10.1 copy.86
  1234.3 2.5 stack_reshape.30
  1238.3 23.2 %copy.90 = bf16[2,2,1024,16,16]{3,4,1,0,2:T(8,128)(2,1)} copy(bf16[2,2,1024,16,16]{2,4,3,1,0:T(8,128)(2,1)S(1)} %pad_maximum_fusion.4) | data formatting | bytes 4194304 | tf_op jit(solution)/shard_map/stack | solution.py:98
  1261.6 13.4 %fusion.9 = bf16[2,1024,16,16]{2,3,0,1:T(8,128)(2,1)} fusion(bf16[2,2,1024,16,16]{3,4,1,0,2:T(8,128)(2,1)} %copy.90, bf16[2,1024,16,16,1]{3,2,0,4,1:T(8,128)(2,1)} %copy.94), kind=kOutput, calls=%fused_computation.28 | convolution fusion | flops 34078720 | bytes 4194304 | tf_op jit(solution)/shard_map/cfws,kcfwt->kfst/dot_general | solution.py:99
  1275.0 10.1 copy.92
  1285.1 4.0 fusion.10
  (176 shorter events, 99.5 us)
Async XLA Ops:
  0.0 1.5 copy-start
  0.0 47.7 %copy-start.10 = (s32[4,16]{1,0:T(4,128)S(1)}, s32[4,16]{1,0:T(4,128)}, u32[]{:S(2)}) copy-start(s32[4,16]{1,0:T(4,128)} %param.11) | copy-start | bytes 772
  0.0 47.8 %copy-start.2 = (bf16[256]{0:T(256)(128)(2,1)S(1)}, bf16[256]{0:T(256)(128)(2,1)}, u32[]{:S(2)}) copy-start(bf16[256]{0:T(256)(128)(2,1)} %param.8) | copy-start | bytes 1540
  3.6 817.7 %all-to-all-start = ((bf16[16,16,1024]{2,1,0:T(8,128)(2,1)}), bf16[16,16,1024]{2,1,0:T(8,128)(2,1)S(1)}, u32[]{:S(2)}, u32[]{:S(2)}) async-start(bf16[16,16,1024]{2,1,0:T(8,128)(2,1)} %broadcast_select_fusion.4), calls=%async_computation | async-start | bytes 1048576 | tf_op jit(solution)/shard_map/all_to_all | solution.py:108
  860.5 6.4 collective-permute-start
  860.8 7.1 collective-permute-start.1
  862.4 9.5 collective-permute-start.2
  864.6 7.9 collective-permute-start.3
  866.1 13.2 %collective-permute-start.4 = (bf16[1,2,64,256]{3,2,1,0:T(8,128)(2,1)S(1)}, bf16[1,2,64,256]{3,2,1,0:T(8,128)(2,1)S(1)}, u32[]{:S(2)}, u32[]{:S(2)}) collective-permute-start(bf16[1,2,64,256]{3,2,1,0:T(8,128)(2,1)S(1)} %get-tuple-element.48), channel_id=1, source_target_pairs={{0,5},{1,6},{2,7},{3,8},{4,9},{5,10},{6,11},{7,12},{8,13},{9,14},{... | collective-permute-start | bytes 196616 | tf_op jit(solution)/shard_map/ppermute | solution.py:125
  866.9 12.6 collective-permute-start.5
  867.8 12.1 collective-permute-start.6
  871.9 11.2 collective-permute-start.7
  872.5 11.4 collective-permute-start.8
  879.3 7.3 collective-permute-start.9
  879.5 8.3 collective-permute-start.10
  879.9 7.9 collective-permute-start.11
  883.0 4.9 collective-permute-start.12
  883.9 6.2 collective-permute-start.13
  886.6 3.5 collective-permute-start.14
  890.1 1.0 copy-start.6
  896.9 29.0 %all-to-all-start.1 = ((bf16[16,2,64,256]{3,2,1,0:T(8,128)(2,1)}), bf16[16,2,64,256]{3,2,1,0:T(8,128)(2,1)}, u32[]{:S(2)}, u32[]{:S(2)}) async-start(bf16[16,2,64,256]{3,2,1,0:T(8,128)(2,1)} %broadcast_select_fusion.3), calls=%async_computation.1 | async-start | bytes 2097152 | tf_op jit(solution)/shard_map/all_to_all | solution.py:133
  925.9 29.9 %all-to-all-start.2 = ((bf16[16,2,64,256]{3,2,1,0:T(8,128)(2,1)}), bf16[16,2,64,256]{3,2,1,0:T(8,128)(2,1)}, u32[]{:S(2)}, u32[]{:S(2)}) async-start(bf16[16,2,64,256]{3,2,1,0:T(8,128)(2,1)} %broadcast_select_fusion.2), calls=%async_computation.2 | async-start | bytes 2097152 | tf_op jit(solution)/shard_map/all_to_all | solution.py:133
  955.8 29.9 %all-to-all-start.3 = ((bf16[16,2,64,256]{3,2,1,0:T(8,128)(2,1)}), bf16[16,2,64,256]{3,2,1,0:T(8,128)(2,1)}, u32[]{:S(2)}, u32[]{:S(2)}) async-start(bf16[16,2,64,256]{3,2,1,0:T(8,128)(2,1)} %broadcast_select_fusion.1), calls=%async_computation.3 | async-start | bytes 2097152 | tf_op jit(solution)/shard_map/all_to_all | solution.py:133
  985.7 47.8 %all-to-all-start.4 = ((bf16[16,2,64,256]{3,2,1,0:T(8,128)(2,1)}), bf16[16,2,64,256]{3,2,1,0:T(8,128)(2,1)S(1)}, u32[]{:S(2)}, u32[]{:S(2)}) async-start(bf16[16,2,64,256]{3,2,1,0:T(8,128)(2,1)} %broadcast_select_fusion), calls=%async_computation.4 | async-start | bytes 2097152 | tf_op jit(solution)/shard_map/all_to_all | solution.py:133
  1090.8 21.1 %copy-start.5 = (bf16[1,2,16,64,256]{3,2,4,1,0:T(8,128)(2,1)S(1)}, bf16[1,2,16,64,256]{3,2,4,1,0:T(8,128)(2,1)}, u32[]{:S(2)}) copy-start(bf16[1,2,16,64,256]{3,2,4,1,0:T(8,128)(2,1)} %copy.75) | copy-start | bytes 3145732
  1153.6 21.3 %copy-start.4 = (bf16[1,2,16,64,256]{3,2,4,1,0:T(8,128)(2,1)S(1)}, bf16[1,2,16,64,256]{3,2,4,1,0:T(8,128)(2,1)}, u32[]{:S(2)}) copy-start(bf16[1,2,16,64,256]{3,2,4,1,0:T(8,128)(2,1)} %copy.81) | copy-start | bytes 3145732
  1216.5 17.7 %copy-start.3 = (bf16[1,2,16,64,256]{3,2,4,1,0:T(8,128)(2,1)S(1)}, bf16[1,2,16,64,256]{3,2,4,1,0:T(8,128)(2,1)}, u32[]{:S(2)}) copy-start(bf16[1,2,16,64,256]{3,2,4,1,0:T(8,128)(2,1)} %copy.87) | copy-start | bytes 3145732
  1275.0 10.1 copy-start.7
  1275.0 10.1 copy-start.8
  1275.0 10.1 copy-start.9
  1285.1 4.0 copy-start.1
